TPU v7x, 32 devices: a whole 2x2x4 slice. The times are simulated.
32 devices in a mesh: ctx: 8 (over z, x), tp: 4 (over y, core).
Axes of the slice: x: 2, y: 2, z: 4, core: 2. Of those that a mesh axis runs over, the one named last changes fastest.
Arguments:
- x_in: bfloat16 [4096, 4096], P('ctx', 'tp'), may hold values from -6 to 6
- bc_in: bfloat16 [4096, 256], P('ctx'), may hold values from -6 to 6
- z_in: bfloat16 [4096, 4096], P('ctx', 'tp'), may hold values from -6 to 6
- codes: int32 [4096, 32], P('ctx', 'tp'), may hold values from 0 to 63
- head_rate: float32 [32], P('tp'), may hold values from 0.25 to 1
- conv_x: float32 [4, 4096], P(None, 'tp'), may hold values from -3 to 3
- conv_bc: float32 [4, 256], replicated, may hold values from -3 to 3
- bias_x: float32 [4096], P('tp'), may hold values from -2 to 2
- bias_bc: float32 [256], replicated, may hold values from -2 to 2
- skip: float32 [32], P('tp'), may hold values from 0.5 to 1.5
- norm_gain: float32 [4096], P('tp'), may hold values from 0.5 to 1.5
- w_out: bfloat16 [4096, 8192], P('tp'), may hold values from -0.125 to 0.125
Outputs:
- mixed: bfloat16 [4096, 8192], P('ctx', 'tp')
All inputs are finite; a program needn't handle non-finite values.
Results may differ from a plain program's by a relative error of at most 0.019.
Values may be sent and summed in bfloat16 or wider, within the bound.
A program may use at most 128 MiB of HBM per device.

v0:
```python
import math

import jax
import jax.numpy as jnp
from jax import lax
from jax.sharding import PartitionSpec as P


def shifted(value, axis, steps):
    count = lax.axis_size(axis)
    first, last = (max(0, -steps), min(count, count - steps))
    return lax.ppermute(value, axis, [(source, source + steps) for source in range(first, last)])


def carried_in(shard, axis, join, neutral):
    place = lax.axis_index(axis)
    gathered = jax.tree.map(
        lambda a, kind: lax.all_gather(a.astype(kind), axis), shard, (jnp.bfloat16, jnp.bfloat16)
    )
    state = jax.tree.map(lambda a, e: jnp.zeros_like(a) + jnp.asarray(e, a.dtype), shard, neutral)

    def one(lap, state):
        return join(
            state,
            jax.tree.map(
                lambda a, own: lax.dynamic_index_in_dim(a, lap, 0, False).astype(own.dtype),
                gathered,
                shard,
            ),
        )

    return lax.fori_loop(0, place, one, state)


def causal_conv(signal, rim_rows, weight, shift_bias):
    tok_count = signal.shape[0]
    extended = jnp.concatenate([rim_rows, signal], axis=0).astype(jnp.float32)
    total = shift_bias[None, :]
    for k in range(4):
        total = total + weight[k][None, :] * extended[k : k + tok_count]
    return jax.nn.silu(total).astype(jnp.bfloat16)


def body(
    x_in, bc_in, z_in, codes, head_rate, conv_x, conv_bc, bias_x, bias_bc, skip, norm_gain, w_out
):
    wide = lax.Precision.HIGH
    tok_rows = x_in.shape[0]
    head_count = skip.shape[0]
    head_width = x_in.shape[1] // head_count
    state_dim = bc_in.shape[1] // 2
    seq_total = tok_rows * lax.axis_size("ctx")
    rim_x, rim_bc = shifted((x_in[tok_rows - 3 :], bc_in[tok_rows - 3 :]), "ctx", 1)
    xc = causal_conv(x_in, rim_x, conv_x, bias_x).reshape(tok_rows, head_count, head_width)
    bcc = causal_conv(bc_in, rim_bc, conv_bc, bias_bc)
    in_maps = bcc[:, :state_dim]
    out_maps = bcc[:, state_dim:]
    log_decay = -12.288 / seq_total * head_rate[None, :] * codes.astype(jnp.float32) / 63.0
    local_cum = jnp.cumsum(log_decay, axis=0)
    block_len = math.gcd(tok_rows, 128)
    causal = jnp.tril(jnp.ones((block_len, block_len), dtype=bool))[:, :, None]
    running_state = jnp.zeros((head_count, state_dim, head_width), jnp.float32)
    block_start = jnp.zeros((head_count,), jnp.float32)
    outputs = []
    for index in range(tok_rows // block_len):
        lower = index * block_len
        x_block = xc[lower : lower + block_len]
        in_block = in_maps[lower : lower + block_len]
        out_block = out_maps[lower : lower + block_len]
        cum_block = local_cum[lower : lower + block_len]
        scores = jnp.dot(out_block, in_block.T, preferred_element_type=jnp.float32)
        log_gap = cum_block[:, None, :] - cum_block[None, :, :]
        weights = (
            jnp.where(causal, jnp.exp(jnp.where(causal, log_gap, 0.0)), 0.0) * scores[:, :, None]
        )
        weights = weights.astype(jnp.bfloat16)
        inside = jnp.einsum("tsh,shp->thp", weights, x_block, preferred_element_type=jnp.float32)
        carried = jnp.einsum(
            "tn,hnp->thp", out_block.astype(jnp.float32), running_state, precision=wide
        )
        carried = carried * jnp.exp(cum_block - block_start[None, :])[:, :, None]
        outputs.append(inside + carried)
        block_end = cum_block[-1]
        factors = jnp.exp(block_end[None, :] - cum_block)
        sent = (x_block.astype(jnp.float32) * factors[:, :, None]).astype(jnp.bfloat16)
        added = jnp.einsum("sn,shp->hnp", in_block, sent, preferred_element_type=jnp.float32)
        running_state = jnp.exp(block_end - block_start)[:, None, None] * running_state + added
        block_start = block_end
    scanned = jnp.concatenate(outputs, axis=0)
    decay_total = local_cum[-1]
    empty_state = jnp.zeros((head_count, state_dim, head_width), jnp.float32)

    def combine_pair(earlier, latter):
        return (earlier[0] + latter[0], jnp.exp(latter[0])[:, None, None] * earlier[1] + latter[1])

    identity = (jnp.zeros((head_count,), jnp.float32), empty_state)
    _, incoming = carried_in((decay_total, running_state), "ctx", combine_pair, identity)
    from_before = jnp.einsum("tn,hnp->thp", out_maps.astype(jnp.float32), incoming, precision=wide)
    from_before = from_before * jnp.exp(local_cum)[:, :, None]
    ssd_scale = 1.0 / math.sqrt(state_dim * seq_total)
    ssd = (scanned + from_before) * ssd_scale + skip[None, :, None] * xc.astype(jnp.float32)
    gated_out = ssd * jax.nn.silu(
        z_in.astype(jnp.float32).reshape(tok_rows, head_count, head_width)
    )
    mean_square = jnp.mean(gated_out * gated_out, axis=-1, keepdims=True)
    normed = (
        gated_out * lax.rsqrt(mean_square + 1e-05) * norm_gain.reshape(head_count, head_width)[None]
    )
    normed = normed.astype(jnp.bfloat16).reshape(tok_rows, head_count * head_width)
    partial_value = jnp.dot(normed, w_out, preferred_element_type=jnp.float32)
    summed = lax.psum_scatter(
        partial_value.astype(jnp.bfloat16), "tp", scatter_dimension=1, tiled=True
    )
    return summed


def solution(mesh):
    in_specs = (
        P("ctx", "tp"),
        P("ctx", None),
        P("ctx", "tp"),
        P("ctx", "tp"),
        P("tp"),
        P(None, "tp"),
        P(),
        P("tp"),
        P(),
        P("tp"),
        P("tp"),
        P("tp", None),
    )
    out_specs = P("ctx", "tp")
    return jax.shard_map(body, mesh=mesh, in_specs=in_specs, out_specs=out_specs, check_vma=False)
```

profile of v0, /device:TPU:27, one launch (start us, length us, event | category | flops | bytes accessed | tf_op | source)
XLA Modules:
  0.0 195.5 jit_solution(15033518266602836789)
XLA Ops:
  7.3 1.3 collective-permute-start.1
  9.5 1.3 collective-permute-start
  13.1 1.1 reduce-window.6
  16.9 1.5 copy.75
  19.8 2.8 %multiply_convert_fusion.1 = bf16[512,1024]{0,1:T(8,128)(2,1)S(1)} fusion(f32[515,1024]{0,1:T(8,128)S(1)} %maximum_convert_fusion, f32[1024]{0:T(1024)S(1)} %bitcast.127, f32[1024]{0:T(1024)S(1)} %bitcast.128, f32[1024]{0:T(1024)S(1)} %bitcast.126, f32[1024]{0:T(1024)S(1)} %bitcast.125, f32[1024]{0:T(1024)S(1)} %copy-done.16), kind=kLoop, calls=%fused_computation.17 | loop fusion | flops 6815744 | bytes 9457664 | tf_op jit(solution)/shard_map/convert_element_type | solution.py:41
  24.8 1.8 copy.83
  26.9 13.4 %all-gather.1 = bf16[8,1,8]{2,1,0:T(2,128)(2,1)S(1)} all-gather(bf16[1,1,8]{2,1,0:T(2,128)(2,1)S(1)} %bitcast.135), channel_id=1, replica_groups=mesh['ctx'=8,'tp'=4] {'ctx'}, dimensions={0}, use_global_device_ids=true | all-gather | bytes 144 | tf_op jit(solution)/shard_map/all_gather | solution.py:18
  40.8 2.3 %copy.87 = bf16[512,1024]{0,1:T(8,128)(2,1)} copy(bf16[512,1024]{1,0:T(8,128)(2,1)} %param.16) | data formatting | bytes 2097152 | tf_op args[2]
  43.1 2.6 %copy.89 = f32[512,8,128]{2,0,1:T(8,128)} copy(bf16[512,8,128]{0,2,1:T(8,128)(2,1)} %bitcast.113) | data formatting | bytes 3145728 | tf_op jit(solution)/shard_map/reshape | solution.py:103
  47.6 1.7 convolution_multiply_fusion.3
  49.3 1.6 copy.86
  53.4 1.1 fusion.11
  54.5 1.1 fusion.12
  55.7 1.1 fusion.13
  56.8 1.1 fusion.14
  57.9 19.6 %all-gather.4.cloned.1.call-done = bf16[64,128,128]{2,1,0:T(8,128)(2,1)} async-done(((bf16[8,128,128]{2,1,0:T(8,128)(2,1)}), bf16[64,128,128]{2,1,0:T(8,128)(2,1)}) %all-gather.4.cloned.1.call-update) | async-done | bytes 2097168 | tf_op jit(solution)/shard_map/all_gather | solution.py:18
  77.6 12.9 %while.12 = (s32[]{:T(128)}, f32[8,128,128]{2,1,0:T(8,128)S(1)}, s32[]{:T(128)}, bf16[8,8]{1,0:T(8,128)(2,1)}, bf16[8,8,128,128]{3,2,1,0:T(8,128)(2,1)}, /*index=5*/s32[]{:T(128)}, s32[]{:T(128)}, s32[]{:T(128)}) while((s32[]{:T(128)}, f32[8,128,128]{2,1,0:T(8,128)S(1)}, s32[]{:T(128)}, bf16[8,8]{1,0:T(8,128)(2,1)}, ...), condition=%wide.region_3.4_spmd, body=%wide.region_2.3_spmd.sunk | while | flops 393229 | bytes 1310935 | solution.py:32
  78.3 1.1 convert_add_fusion.2
  80.1 1.1 convert_add_fusion.2
  89.2 1.1 convert_add_fusion.2
  91.4 1.9 copy.85
  93.3 4.1 %multiply_reduce_fusion = (f32[512,8]{0,1:T(8,128)S(1)}, f32[512,8,128]{2,0,1:T(8,128)S(1)}) fusion(f32[512,8,128]{2,0,1:T(8,128)} %copy.89, f32[512,8,128]{2,0,1:T(8,128)} %copy.86, f32[8]{0:T(128)S(1)} %copy-done.19, f32[512,8,128]{2,0,1:T(8,128)} %copy.85, f32[512,8]{0,1:T(8,128)S(1)} %copy-done.10, f32[128,8,128]{2,0,1:T(8,128)} %fusion.14, ...), kind=kLoop, calls=%fused_computation.16 | loop fusion | flops 7860224 | bytes 10518560 | tf_op jit(solution)/shard_map/reduce_sum | solution.py:105
  98.7 17.0 %convolution_convert_fusion = bf16[512,8192]{1,0:T(8,128)(2,1)} fusion(bf16[512,1024]{0,1:T(8,128)(2,1)S(1)} %bitcast.123, bf16[1024,8192]{1,0:T(8,128)(2,1)} %param.25), kind=kOutput, calls=%fused_computation.2 | convolution fusion | flops 8594128896 | bytes 26214400 | tf_op jit(solution)/shard_map/dot_general | solution.py:110
  115.7 72.9 %reduce-scatter.2.cloned.1.call-done = bf16[512,2048]{1,0:T(8,128)(2,1)} async-done(((bf16[512,8192]{1,0:T(8,128)(2,1)}), bf16[512,2048]{1,0:T(8,128)(2,1)}) %reduce-scatter.2.cloned.1.call-update) | async-done | bytes 2097168 | tf_op jit(solution)/shard_map/reduce_scatter | solution.py:111
  (95 shorter events, 26.7 us)
Async XLA Ops:
  6.5 11.9 %copy-start.7 = (bf16[512,256]{1,0:T(8,128)(2,1)S(1)}, bf16[512,256]{1,0:T(8,128)(2,1)}, u32[]{:S(2)}) copy-start(bf16[512,256]{1,0:T(8,128)(2,1)} %param.15) | copy-start | bytes 786436
  6.5 12.0 %copy-start.18 = (f32[256]{0:T(256)S(1)}, f32[256]{0:T(256)}, u32[]{:S(2)}) copy-start(f32[256]{0:T(256)} %param.22) | copy-start | bytes 3076
  6.5 71.0 %all-gather.4.cloned.1.call-start = ((), (), s32[]{:S(2)}) async-start(), calls=%async_computation.2 | async-start | bytes 2359296 | tf_op jit(solution)/shard_map/all_gather | solution.py:18
  7.3 11.1 %collective-permute-start.1 = (bf16[3,256]{1,0:T(4,128)(2,1)S(1)}, bf16[3,256]{1,0:T(4,128)(2,1)S(1)}, u32[]{:S(2)}, u32[]{:S(2)}) collective-permute-start(bf16[3,256]{1,0:T(4,128)(2,1)S(1)} %slice.164), channel_id=1, source_target_pairs={{0,4},{4,8},{8,12},{12,16},{16,20},{20,24},{24,28},{1,5},{5,9},{9,... | collective-permute-start | bytes 4616 | tf_op jit(solution)/shard_map/ppermute | solution.py:12
  9.5 9.7 %collective-permute-start = (bf16[3,1024]{0,1:T(8,128)(2,1)S(1)}, bf16[3,1024]{0,1:T(8,128)(2,1)S(1)}, u32[]{:S(2)}, u32[]{:S(2)}) collective-permute-start(bf16[3,1024]{0,1:T(8,128)(2,1)S(1)} %copy.74), channel_id=1, source_target_pairs={{0,4},{4,8},{8,12},{12,16},{16,20},{20,24},{24,28},{1,5},{5,9},{9,... | collective-permute-start | bytes 18440 | tf_op jit(solution)/shard_map/ppermute | solution.py:12
  18.9 0.9 copy-start.16
  22.7 0.7 copy-start.2
  22.8 1.1 copy-start
  26.6 162.0 %reduce-scatter.2.cloned.1.call-start = ((), (), s32[]{:S(2)}) async-start(), calls=%async_computation.1 | async-start | bytes 10485760 | tf_op jit(solution)/shard_map/reduce_scatter | solution.py:111
  50.9 2.1 %copy-start.15 = (f32[128,8]{0,1:T(8,128)S(1)}, f32[128,8]{0,1:T(8,128)}, u32[]{:S(2)}) copy-start(f32[128,8]{0,1:T(8,128)} %get-tuple-element.103) | copy-start | bytes 12292
  50.9 2.4 %copy-start.3 = (bf16[128,1024]{0,1:T(8,128)(2,1)S(1)}, bf16[128,1024]{0,1:T(8,128)(2,1)}, u32[]{:S(2)}) copy-start(bf16[128,1024]{0,1:T(8,128)(2,1)} %copy-done.2) | copy-start | bytes 786436
  50.9 2.4 %copy-start.4 = (f32[128,8,128]{2,0,1:T(8,128)S(1)}, f32[128,8,128]{2,0,1:T(8,128)}, u32[]{:S(2)}) copy-start(f32[128,8,128]{2,0,1:T(8,128)} %convolution_multiply_fusion.3) | copy-start | bytes 1572868
  50.9 2.5 %copy-start.9 = (f32[128,128]{1,0:T(8,128)S(1)}, f32[128,128]{1,0:T(8,128)}, u32[]{:S(2)}) copy-start(f32[128,128]{1,0:T(8,128)} %fusion.71) | copy-start | bytes 196612
  50.9 2.5 %copy-start.14 = (f32[128,8]{0,1:T(8,128)S(1)}, f32[128,8]{0,1:T(8,128)}, u32[]{:S(2)}) copy-start(f32[128,8]{0,1:T(8,128)} %get-tuple-element.98) | copy-start | bytes 12292
  50.9 3.6 %copy-start.8 = (f32[128,128]{1,0:T(8,128)S(1)}, f32[128,128]{1,0:T(8,128)}, u32[]{:S(2)}) copy-start(f32[128,128]{1,0:T(8,128)} %fusion.66) | copy-start | bytes 196612
  50.9 3.6 %copy-start.13 = (f32[128,8]{0,1:T(8,128)S(1)}, f32[128,8]{0,1:T(8,128)}, u32[]{:S(2)}) copy-start(f32[128,8]{0,1:T(8,128)} %get-tuple-element.96) | copy-start | bytes 12292
  53.0 2.7 %copy-start.12 = (f32[128,8]{0,1:T(8,128)S(1)}, f32[128,8]{0,1:T(8,128)}, u32[]{:S(2)}) copy-start(f32[128,8]{0,1:T(8,128)} %get-tuple-element.105) | copy-start | bytes 12292
  53.3 3.4 %copy-start.1 = (bf16[128,1024]{0,1:T(8,128)(2,1)S(1)}, bf16[128,1024]{0,1:T(8,128)(2,1)}, u32[]{:S(2)}) copy-start(bf16[128,1024]{0,1:T(8,128)(2,1)} %copy-done) | copy-start | bytes 786436
  53.3 3.4 %copy-start.11 = (f32[128,8]{0,1:T(8,128)S(1)}, f32[128,8]{0,1:T(8,128)}, u32[]{:S(2)}) copy-start(f32[128,8]{0,1:T(8,128)} %get-tuple-element.104) | copy-start | bytes 12292
  91.4 1.9 copy-start.5
  91.4 1.9 copy-start.6
  91.4 1.9 copy-start.10
  91.4 1.9 copy-start.19
  93.3 4.1 %copy-start.17 = (f32[1024]{0:T(1024)S(1)}, f32[1024]{0:T(1024)}, u32[]{:S(2)}) copy-start(f32[1024]{0:T(1024)} %param.24) | copy-start | bytes 12292
Sparse Core Ops, SparseCore 0:
  26.7 50.7 all-gather.3
  115.8 72.7 reduce-scatter.1
where the time goes:
time: 198 us; the launch traced here: 195 us
  waiting for transfers between devices  92.9 us (47%)
  matrix products  29.7 us (15%)
  other arithmetic  25.1 us (13%)
  local copies, waits for them, and re-layouts  17.6 us (9%)
  between operations  13.8 us (7%)
  blocking collectives  13.4 us (7%)
  starting transfers between devices  2.62 us (1%)
    reduce_scatter x1, waiting for transfers between devices, body(): lax.psum_scatter(partial_value.astype(jnp.bfloat16), 'tp', scatter_dimens...  72.9 us
    all_gather x1, waiting for transfers between devices, carried_in(): lax.all_gather(a.astype(kind), axis)  19.6 us
    dot_general x1, matrix products, body(): partial_value = jnp.dot(normed, w_out, preferred_element_type=jnp.float32)  17 us
    all_gather x1, blocking collectives, carried_in(): lax.all_gather(a.astype(kind), axis)  13.4 us
    add x7, other arithmetic, combine_pair(): jnp.exp(latter[0])[:, None, None] * earlier[1] + latter[1]  7.75 us
    unnamed x43, local copies, waits for them, and re-layouts  4.9 us
    exp x7, other arithmetic, combine_pair(): jnp.exp(latter[0])[:, None, None] * earlier[1] + latter[1]  4.8 us
    dot_general x4, matrix products, body(): jnp.einsum('tsh,shp->thp', weights, x_block, preferred_element_type=jnp.f...  4.54 us
  transfers between devices with their start and end apart: 4, of which 3 were waited for; matrix products, arithmetic and copies ran while one was open for 14% of the time, Pallas kernels for 0%

commit v1 on v0

v1 whole, which is shorter than its diff:
```python
import functools
import math

import jax
import jax.numpy as jnp
from jax import lax
from jax.experimental import pallas as pl
from jax.experimental.pallas import tpu as pltpu
from jax.sharding import PartitionSpec as P

MESH = pl.DeviceIdType.MESH
F32 = jnp.float32
BF16 = jnp.bfloat16
BLOCK = 128
GROUP = 256
RIM = 16


def silu(v):
    return v / (1.0 + jnp.exp(-v))


def conv(window, taps, bias):
    total = bias + taps[3:4] * window[RIM:]
    for k in range(3):
        total = total + taps[k : k + 1] * pltpu.roll(window, 3 - k, 0)[RIM:]
    return silu(total).astype(BF16)


def layer(
    n_ctx,
    n_tp,
    n_x,
    x_ref, bc_ref, z_ref, codes_ref, rate_ref, cx_ref, cbc_ref, bx_ref, bbc_ref, skip_ref, gain_ref, w_ref,
    out_ref,
    rim_x, rim_bc, tril, coded, coef, skips, ec, en, bcc, bt, xc, us, states, pz, pz_next, pin,
    g_all, h_all, own_n, sib_n, w_own, w_sib, y_send, y_recv, local,
    rim_send, rim_recv, wl_sem, ws_send, ws_recv, x_send, x_recv, z_send, z_recv, n_send, n_recv, ys_send, ys_recv,
):
    toks, width = x_ref.shape
    heads = skip_ref.shape[0]
    n_z = n_ctx // n_x
    n_y = n_tp // 2
    blocks = toks // BLOCK
    groups = width // GROUP
    owned = out_ref.shape[1]
    part = y_send.shape[3]
    parts = owned // part
    ctx = lax.axis_index("ctx")
    tp = lax.axis_index("tp")
    iz, ix = ctx // n_x, ctx % n_x
    iy, core = tp // 2, tp % 2
    sib = tp + 1 - 2 * core
    seq = toks * n_ctx
    n_state = bc_ref.shape[1] // 2

    barrier = pltpu.get_barrier_semaphore()

    def greet(c, t):
        pl.semaphore_signal(barrier, inc=1, device_id=(c, t), device_id_type=MESH)

    greet(ctx, sib)
    for r in range(1, n_y):
        greet(ctx, (iy + r) % n_y * 2 + core)
    for r in range(1, n_x):
        greet(iz * n_x + (ix + r) % n_x, tp)
    for near, far in ((ctx > 0, ctx - 1), (ctx < n_ctx - 1, ctx + 1), (iz > 0, ctx - n_x), (iz < n_z - 1, ctx + n_x)):
        pl.when(near)(functools.partial(greet, far, tp))
    count = n_y + n_x - 1
    for near in (ctx > 0, ctx < n_ctx - 1, iz > 0, iz < n_z - 1):
        count = count + jnp.where(near, 1, 0)
    pl.semaphore_wait(barrier, count)

    def remote(src, dst, send, recv, c, t):
        return pltpu.make_async_remote_copy(
            src_ref=src, dst_ref=dst, send_sem=send, recv_sem=recv, device_id=(c, t), device_id_type=MESH
        )

    rims = [
        remote(x_ref.at[pl.ds(toks - RIM, RIM)], rim_x, rim_send.at[0], rim_recv.at[0], ctx + 1, tp),
        remote(bc_ref.at[pl.ds(toks - RIM, RIM)], rim_bc, rim_send.at[1], rim_recv.at[1], ctx + 1, tp),
    ]

    @pl.when(ctx < n_ctx - 1)
    def _():
        for copy in rims:
            copy.start()

    order = list(range(1, n_y)) + [0]
    w_loads, w_swaps = {}, {}
    for r in order:
        chip = (iy + r) % n_y
        mine = pl.ds(pl.multiple_of((chip * 2 + core) * owned, GROUP), owned)
        theirs = pl.ds(pl.multiple_of((chip * 2 + 1 - core) * owned, GROUP), owned)
        w_loads[r] = pltpu.make_async_copy(w_ref.at[:, mine], w_own.at[r], wl_sem.at[r])
        w_swaps[r] = remote(w_ref.at[:, theirs], w_sib.at[r], ws_send.at[r], ws_recv.at[r], ctx, sib)
        w_loads[r].start()
        w_swaps[r].start()

    row_id = lax.broadcasted_iota(jnp.int32, (toks, toks), 0)
    col_id = lax.broadcasted_iota(jnp.int32, (toks, toks), 1)
    tril[...] = jnp.where(row_id >= col_id, 1.0, 0.0).astype(BF16)
    codes = codes_ref[...].astype(F32)
    for h in range(heads):
        cols = slice(h * BLOCK, (h + 1) * BLOCK)
        coded[:, cols] = jnp.broadcast_to(codes[:, h : h + 1], (toks, BLOCK)).astype(BF16)
        coef[:, cols] = jnp.full((8, BLOCK), rate_ref[h] * (-12.288 / seq / 63.0), F32)
        skips[:, cols] = jnp.full((8, BLOCK), skip_ref[h], F32)

    def decays(j, _):
        cols = pl.ds(pl.multiple_of(j * GROUP, GROUP), GROUP)
        cum = jnp.dot(tril[...], coded[:, cols], preferred_element_type=F32) * coef[0:1, cols]
        ec[:, cols] = jnp.exp(cum)
        en[:, cols] = jnp.exp(-cum)
        return 0

    lax.fori_loop(0, groups, decays, 0)

    def conv_x(j, b):
        cols = pl.ds(pl.multiple_of(j * BLOCK, BLOCK), BLOCK)
        rows = pl.ds(b * BLOCK, BLOCK)
        if b == 0:
            window = jnp.concatenate([rim_x[:, cols], x_ref[rows, cols]], axis=0)
        else:
            window = x_ref[pl.ds(b * BLOCK - RIM, BLOCK + RIM), cols]
        value = conv(window.astype(F32), cx_ref[:, cols], bx_ref[:, cols])
        xc[rows, cols] = value
        us[rows, cols] = (value.astype(F32) * en[rows, cols]).astype(BF16)

    def conv_bc(b):
        rows = pl.ds(b * BLOCK, BLOCK)
        if b == 0:
            window = jnp.concatenate([rim_bc[...], bc_ref[rows, :]], axis=0)
        else:
            window = bc_ref[pl.ds(b * BLOCK - RIM, BLOCK + RIM), :]
        value = conv(window.astype(F32), cbc_ref[...], bbc_ref[...])
        bcc[rows, :] = value
        bt[:, b * BLOCK : (b + 1) * BLOCK] = value[:, :n_state].astype(F32).T.astype(BF16)

    def later_blocks(j, _):
        for b in range(1, blocks):
            conv_x(j, b)
        return 0

    def first_block(j, _):
        conv_x(j, 0)
        return 0

    for b in range(1, blocks):
        conv_bc(b)
    lax.fori_loop(0, width // BLOCK, later_blocks, 0)

    @pl.when(ctx == 0)
    def _():
        rim_x[...] = jnp.zeros_like(rim_x)
        rim_bc[...] = jnp.zeros_like(rim_bc)

    @pl.when(ctx > 0)
    def _():
        for copy in rims:
            copy.wait_recv()

    conv_bc(0)
    lax.fori_loop(0, width // BLOCK, first_block, 0)

    x_copies = {}
    for g in range(groups):
        cols = slice(g * GROUP, (g + 1) * GROUP)
        total = ec[toks - 1 : toks, cols]
        state = jnp.dot(bt[...], us[:, cols], preferred_element_type=F32)
        states[n_x - 1, :n_state, cols] = (state * total).astype(BF16)
        high = total.astype(BF16).astype(F32)
        pick = lax.broadcasted_iota(jnp.int32, (RIM, GROUP), 0) < 8
        states[n_x - 1, n_state:, cols] = jnp.where(pick, high, total - high).astype(BF16)
        for r in range(1, n_x):
            x_copies[r, g] = remote(
                states.at[n_x - 1, :, pl.ds(g * GROUP, GROUP)],
                states.at[r - 1, :, pl.ds(g * GROUP, GROUP)],
                x_send.at[r - 1, g], x_recv.at[r - 1, g],
                iz * n_x + (ix + r) % n_x, tp,
            )
            x_copies[r, g].start()

    scale = 1.0 / math.sqrt(n_state * seq)
    for b in range(blocks):
        rows = slice(b * BLOCK, (b + 1) * BLOCK)
        upto = (b + 1) * BLOCK
        scores = lax.dot_general(
            bcc[rows, n_state:], bcc[:upto, :n_state], (((1,), (1,)), ((), ())), preferred_element_type=F32
        )
        scores = (scores * tril[rows, :upto].astype(F32)).astype(BF16)

        def inside(j, _, rows=rows, upto=upto, scores=scores):
            cols = pl.ds(pl.multiple_of(j * GROUP, GROUP), GROUP)
            y = jnp.dot(scores, us[:upto, cols], preferred_element_type=F32)
            gate = silu(z_ref[rows, cols].astype(F32))
            decay = ec[rows, cols] * (scale * gate)
            g_all[rows, cols] = y * decay + skips[0:1, cols] * xc[rows, cols].astype(F32) * gate
            h_all[rows, cols] = decay
            return 0

        lax.fori_loop(0, groups, inside, 0)

    @pl.when(iz == 0)
    def _():
        pz[...] = jnp.zeros_like(pz)

    z_copies = []
    for g in range(groups):
        cols = slice(g * GROUP, (g + 1) * GROUP)
        span = pl.ds(g * GROUP, GROUP)
        copy = remote(pz_next.at[:, span], pz.at[:, span], z_send.at[g], z_recv.at[g], ctx + n_x, tp)
        z_copies.append(copy)
        for r in range(1, n_x):
            x_copies[r, g].wait_recv()
        pl.when(iz > 0)(copy.wait_recv)
        before = pz[:, cols].astype(F32)
        arrived = before
        for k in range(n_x):
            slot = (ix - k - 1 + n_x) % n_x
            arrived = jnp.where(ix == k, before, arrived)
            factor = states[slot, n_state : n_state + 1, cols].astype(F32)
            factor = factor + states[slot, n_state + 8 : n_state + 9, cols].astype(F32)
            before = before * factor + states[slot, :n_state, cols].astype(F32)
        pz_next[:, cols] = before.astype(BF16)
        pl.when(iz < n_z - 1)(copy.start)
        pin[:, cols] = arrived.astype(BF16)

    n_copies = []
    for b in range(blocks):
        span = pl.ds(b * BLOCK, BLOCK)
        n_copies.append(remote(own_n.at[span], sib_n.at[span], n_send.at[b], n_recv.at[b], ctx, sib))

    def norm(b):
        rows = slice(b * BLOCK, (b + 1) * BLOCK)

        def pair(j, _):
            start = pl.multiple_of(j * GROUP, GROUP)
            cols = pl.ds(start, GROUP)
            carried = jnp.dot(bcc[rows, n_state:], pin[:, cols], preferred_element_type=F32)
            gated = g_all[rows, cols] + h_all[rows, cols] * carried
            for half in range(GROUP // BLOCK):
                piece = gated[:, half * BLOCK : (half + 1) * BLOCK]
                mean_square = jnp.mean(piece * piece, axis=-1, keepdims=True)
                cut = pl.ds(pl.multiple_of(start + half * BLOCK, BLOCK), BLOCK)
                own_n[rows, cut] = (piece * lax.rsqrt(mean_square + 1e-05) * gain_ref[:, cut]).astype(BF16)
            return 0

        lax.fori_loop(0, groups, pair, 0)
        n_copies[b].start()

    def project(b, r, first, tiles, store):
        rows = slice(b * BLOCK, (b + 1) * BLOCK)

        def tile(j, _):
            cols = pl.ds(pl.multiple_of(first + j * GROUP, GROUP), GROUP)
            value = jnp.dot(own_n[rows, :], w_own[r, :, cols], preferred_element_type=F32)
            value = value + jnp.dot(sib_n[rows, :], w_sib[r, :, cols], preferred_element_type=F32)
            store(rows, j, cols, value)
            return 0

        lax.fori_loop(0, tiles, tile, 0)

    y_copies = {}

    def send_block(b):
        n_copies[b].wait_recv()
        for r in range(1, n_y):
            if b == 0:
                w_loads[r].wait()
                w_swaps[r].wait_recv()
            for p in range(parts):

                def store(rows, j, cols, value, r=r, p=p):
                    y_send[r - 1, p, rows, pl.ds(pl.multiple_of(j * GROUP, GROUP), GROUP)] = value.astype(BF16)

                project(b, r, p * part, part // GROUP, store)
                span = pl.ds(b * BLOCK, BLOCK)
                at = (b * parts + p,)
                y_copies[b, r, p] = remote(
                    y_send.at[r - 1, p, span], y_recv.at[r - 1, p, span],
                    ys_send.at[r - 1, at[0]], ys_recv.at[r - 1, at[0]],
                    ctx, (iy + r) % n_y * 2 + core,
                )
                y_copies[b, r, p].start()

    norm(0)
    for b in range(blocks):
        if b + 1 < blocks:
            norm(b + 1)
        send_block(b)

    w_loads[0].wait()
    w_swaps[0].wait_recv()

    def keep(rows, j, cols, value):
        local[rows, cols] = value

    for b in range(blocks):
        project(b, 0, 0, owned // GROUP, keep)

    for b in range(blocks):
        rows = slice(b * BLOCK, (b + 1) * BLOCK)
        for p in range(parts):
            cols = slice(p * part, (p + 1) * part)
            total = local[rows, cols]
            for r in range(1, n_y):
                y_copies[b, r, p].wait_recv()
                total = total + y_recv[r - 1, p, rows, :].astype(F32)
            out_ref[rows, cols] = total.astype(BF16)

    @pl.when(ctx < n_ctx - 1)
    def _():
        for copy in rims:
            copy.wait_send()

    @pl.when(iz < n_z - 1)
    def _():
        for copy in z_copies:
            copy.wait_send()

    for copies in (w_swaps.values(), x_copies.values(), n_copies, y_copies.values()):
        for copy in copies:
            copy.wait_send()


def solution(mesh):
    n_ctx, n_tp = mesh.shape["ctx"], mesh.shape["tp"]
    n_x = max(1, n_ctx // 4)

    def body(x_in, bc_in, z_in, codes, head_rate, conv_x, conv_bc, bias_x, bias_bc, skip, norm_gain, w_out):
        toks, width = x_in.shape
        maps = bc_in.shape[1]
        n_state = maps // 2
        depth, model = w_out.shape
        owned = model // n_tp
        part = min(owned, 1024)
        n_y = n_tp // 2
        far = max(1, n_y - 1)
        row = max(1, n_x - 1)
        groups = width // GROUP
        blocks = toks // BLOCK
        vmem = pl.BlockSpec(memory_space=pltpu.VMEM)
        smem = pl.BlockSpec(memory_space=pltpu.SMEM)
        dma = pltpu.SemaphoreType.DMA
        pieces = blocks * (owned // part)
        return pl.pallas_call(
            functools.partial(layer, n_ctx, n_tp, n_x),
            out_shape=jax.ShapeDtypeStruct((toks, owned), BF16),
            in_specs=[vmem, vmem, vmem, vmem, smem, vmem, vmem, vmem, vmem, smem, vmem,
                      pl.BlockSpec(memory_space=pl.ANY)],
            out_specs=vmem,
            scratch_shapes=[
                pltpu.VMEM((RIM, width), BF16),
                pltpu.VMEM((RIM, maps), BF16),
                pltpu.VMEM((toks, toks), BF16),
                pltpu.VMEM((toks, width), BF16),
                pltpu.VMEM((8, width), F32),
                pltpu.VMEM((8, width), F32),
                pltpu.VMEM((toks, width), F32),
                pltpu.VMEM((toks, width), F32),
                pltpu.VMEM((toks, maps), BF16),
                pltpu.VMEM((n_state, toks), BF16),
                pltpu.VMEM((toks, width), BF16),
                pltpu.VMEM((toks, width), BF16),
                pltpu.VMEM((n_x, n_state + RIM, width), BF16),
                pltpu.VMEM((n_state, width), BF16),
                pltpu.VMEM((n_state, width), BF16),
                pltpu.VMEM((n_state, width), BF16),
                pltpu.VMEM((toks, width), F32),
                pltpu.VMEM((toks, width), F32),
                pltpu.VMEM((toks, width), BF16),
                pltpu.VMEM((toks, width), BF16),
                pltpu.VMEM((n_y, depth, owned), BF16),
                pltpu.VMEM((n_y, depth, owned), BF16),
                pltpu.VMEM((far, owned // part, toks, part), BF16),
                pltpu.VMEM((far, owned // part, toks, part), BF16),
                pltpu.VMEM((toks, owned), F32),
                dma((2,)), dma((2,)),
                dma((n_y,)), dma((n_y,)), dma((n_y,)),
                dma((row, groups)), dma((row, groups)),
                dma((groups,)), dma((groups,)),
                dma((blocks,)), dma((blocks,)),
                dma((far, pieces)), dma((far, pieces)),
            ],
            compiler_params=pltpu.CompilerParams(
                collective_id=0, has_side_effects=True, vmem_limit_bytes=60 * 1024 * 1024
            ),
        )(x_in, bc_in, z_in, codes, head_rate, conv_x, conv_bc, bias_x[None], bias_bc[None], skip,
          norm_gain[None], w_out)

    in_specs = (
        P("ctx", "tp"), P("ctx", None), P("ctx", "tp"), P("ctx", "tp"), P("tp"), P(None, "tp"),
        P(), P("tp"), P(), P("tp"), P("tp"), P("tp", None),
    )
    return jax.shard_map(body, mesh=mesh, in_specs=in_specs, out_specs=P("ctx", "tp"), check_vma=False)
```

time: 198 us -> 83 us (0.42); the launches traced: 195 us -> 82.7 us
  waiting for transfers between devices: 92.9 us -> 0 us
  Pallas kernels: 0 us -> 77.9 us
  matrix products: 29.7 us -> 0 us
  other arithmetic: 25.1 us -> 0 us
  between operations: 13.8 us -> 0.01 us
  blocking collectives: 13.4 us -> 0 us
  local copies, waits for them, and re-layouts: 17.6 us -> 4.71 us
  starting transfers between devices: 2.62 us -> 0 us
    pallas_call x0 -> x1, Pallas kernels: none -> 77.9 us  [body(): pl.pallas_call(functools.partial(layer, n_ctx, n_tp, n_x), out_shape=jax....]
    reduce_scatter x1 -> x0, waiting for transfers between devices: 72.9 us -> none  [body(): lax.psum_scatter(partial_value.astype(jnp.bfloat16), 'tp', scatter_dimens...]
    dot_general x17 -> x0, matrix products: 29 us -> none  [the longest x1 17 us: body(): partial_value = jnp.dot(normed, w_out, preferred_element_type=jnp.float32)]
    all_gather x1 -> x0, waiting for transfers between devices: 19.6 us -> none  [carried_in(): lax.all_gather(a.astype(kind), axis)]
    all_gather x1 -> x0, blocking collectives: 13.4 us -> none  [carried_in(): lax.all_gather(a.astype(kind), axis)]
    add x7 -> x0, other arithmetic: 7.75 us -> none  [combine_pair(): jnp.exp(latter[0])[:, None, None] * earlier[1] + latter[1]]
    exp x10 -> x0, other arithmetic: 6.18 us -> none  [the longest x7 4.8 us: combine_pair(): jnp.exp(latter[0])[:, None, None] * earlier[1] + latter[1]]
    convert_element_type x5 -> x0, other arithmetic: 4.45 us -> none  [the longest x2 3.11 us: causal_conv(): return jax.nn.silu(total).astype(jnp.bfloat16)]
  transfers between devices with their start and end apart: 4 -> 0, of which waited for: 3 -> 0; matrix products, arithmetic and copies ran while one was open for 14% -> 0% of each run, Pallas kernels for 0% -> 0%
where the time goes in v1:
time: 83 us; the launch traced here: 82.7 us
  Pallas kernels  77.9 us (94%)
  local copies, waits for them, and re-layouts  4.71 us (6%)
    pallas_call x1, Pallas kernels, body(): pl.pallas_call(functools.partial(layer, n_ctx, n_tp, n_x), out_shape=jax....  77.9 us
    unnamed x2, local copies, waits for them, and re-layouts  4.71 us

profile of v1, /device:TPU:27, one launch (start us, length us, event | category | flops | bytes accessed | tf_op | source)
XLA Modules:
  0.0 82.7 jit_solution(1645996113082162250)
XLA Ops:
  0.0 1.6 %copy.13.codes_ref = s32[512,8]{1,0:T(8,128)} copy(s32[512,8]{0,1:T(8,128)} %param.15) | data formatting | bytes 32768 | tf_op args[3]
  1.6 77.9 %shard_map.118 = bf16[512,2048]{1,0:T(8,128)(2,1)} custom-call(bf16[512,1024]{1,0:T(8,128)(2,1)} %x_ref.1, bf16[512,256]{1,0:T(8,128)(2,1)} %bc_ref.1, bf16[512,1024]{1,0:T(8,128)(2,1)} %z_ref.1, s32[512,8]{1,0:T(8,128)} %copy.13.codes_ref, f32[8]{0:T(128)} %rate_ref.1, f32[4,1024]{1,0:T(4,128)} %cx_ref.1, f32[4,256]{1,0:T(4,128)} %cbc_ref.1, ...), custom_call_target="tpu_custom_call" | custom-call | tf_op jit(solution)/shard_map/pallas_call | solution.py:347
  79.5 3.2 %copy.15 = bf16[512,2048]{1,0:T(8,128)(2,1)} copy(bf16[512,2048]{1,0:T(8,128)(2,1)} %shard_map.118) | data formatting | bytes 4194304

commit v2 on v1

--- a/solution.py
+++ b/solution.py
@@ -31,13 +31,13 @@
     n_ctx,
     n_tp,
     n_x,
-    x_ref, bc_ref, z_ref, codes_ref, rate_ref, cx_ref, cbc_ref, bx_ref, bbc_ref, skip_ref, gain_ref, w_ref,
+    x_hbm, bc_ref, z_hbm, codes_ref, rate_ref, cx_ref, cbc_ref, bx_ref, bbc_ref, skip_ref, gain_ref, w_ref,
     out_ref,
-    rim_x, rim_bc, tril, coded, coef, skips, ec, en, bcc, bt, xc, us, states, pz, pz_next, pin,
+    x_ref, z_ref, pm, rim_x, rim_bc, tril, coded, coef, skips, ec, en, bcc, bt, xc, us, states, pz, pz_next, pin,
     g_all, h_all, own_n, sib_n, w_own, w_sib, y_send, y_recv, local,
-    rim_send, rim_recv, wl_sem, ws_send, ws_recv, x_send, x_recv, z_send, z_recv, n_send, n_recv, ys_send, ys_recv,
+    xl_sem, zl_sem, rim_send, rim_recv, wl_sem, ws_send, ws_recv, x_send, x_recv, z_send, z_recv, n_send, n_recv, ys_send, ys_recv,
 ):
-    toks, width = x_ref.shape
+    toks, width = x_hbm.shape
     heads = skip_ref.shape[0]
     n_z = n_ctx // n_x
     n_y = n_tp // 2
@@ -69,15 +69,37 @@
     count = n_y + n_x - 1
     for near in (ctx > 0, ctx < n_ctx - 1, iz > 0, iz < n_z - 1):
         count = count + jnp.where(near, 1, 0)
-    pl.semaphore_wait(barrier, count)
 
     def remote(src, dst, send, recv, c, t):
         return pltpu.make_async_remote_copy(
             src_ref=src, dst_ref=dst, send_sem=send, recv_sem=recv, device_id=(c, t), device_id_type=MESH
         )
 
+    def span_of(g):
+        return pl.ds(pl.multiple_of(g * GROUP, GROUP), GROUP)
+
+    def load_x(g):
+        return pltpu.make_async_copy(x_hbm.at[:, span_of(g)], x_ref.at[:, span_of(g)], xl_sem.at[g])
+
+    load_z = pltpu.make_async_copy(z_hbm, z_ref, zl_sem.at[0])
+    for g in range(groups):
+        load_x(g).start()
+    load_z.start()
+
+    row_id = lax.broadcasted_iota(jnp.int32, (toks, toks), 0)
+    col_id = lax.broadcasted_iota(jnp.int32, (toks, toks), 1)
+    tril[...] = jnp.where(row_id >= col_id, 1.0, 0.0).astype(BF16)
+    codes = codes_ref[...].astype(F32).T
+    for h in range(heads):
+        cols = slice(h * BLOCK, (h + 1) * BLOCK)
+        coded[:, cols] = jnp.broadcast_to(codes[:, h : h + 1], (toks, BLOCK)).astype(BF16)
+        coef[:, cols] = jnp.full((8, BLOCK), rate_ref[h] * (-12.288 / seq / 63.0), F32)
+        skips[:, cols] = jnp.full((8, BLOCK), skip_ref[h], F32)
+
+    pl.semaphore_wait(barrier, count)
+
     rims = [
-        remote(x_ref.at[pl.ds(toks - RIM, RIM)], rim_x, rim_send.at[0], rim_recv.at[0], ctx + 1, tp),
+        remote(x_hbm.at[pl.ds(toks - RIM, RIM)], rim_x, rim_send.at[0], rim_recv.at[0], ctx + 1, tp),
         remote(bc_ref.at[pl.ds(toks - RIM, RIM)], rim_bc, rim_send.at[1], rim_recv.at[1], ctx + 1, tp),
     ]
 
@@ -97,35 +119,14 @@
         w_loads[r].start()
         w_swaps[r].start()
 
-    row_id = lax.broadcasted_iota(jnp.int32, (toks, toks), 0)
-    col_id = lax.broadcasted_iota(jnp.int32, (toks, toks), 1)
-    tril[...] = jnp.where(row_id >= col_id, 1.0, 0.0).astype(BF16)
-    codes = codes_ref[...].astype(F32)
-    for h in range(heads):
-        cols = slice(h * BLOCK, (h + 1) * BLOCK)
-        coded[:, cols] = jnp.broadcast_to(codes[:, h : h + 1], (toks, BLOCK)).astype(BF16)
-        coef[:, cols] = jnp.full((8, BLOCK), rate_ref[h] * (-12.288 / seq / 63.0), F32)
-        skips[:, cols] = jnp.full((8, BLOCK), skip_ref[h], F32)
-
     def decays(j, _):
-        cols = pl.ds(pl.multiple_of(j * GROUP, GROUP), GROUP)
+        cols = span_of(j)
         cum = jnp.dot(tril[...], coded[:, cols], preferred_element_type=F32) * coef[0:1, cols]
         ec[:, cols] = jnp.exp(cum)
         en[:, cols] = jnp.exp(-cum)
         return 0
 
     lax.fori_loop(0, groups, decays, 0)
-
-    def conv_x(j, b):
-        cols = pl.ds(pl.multiple_of(j * BLOCK, BLOCK), BLOCK)
-        rows = pl.ds(b * BLOCK, BLOCK)
-        if b == 0:
-            window = jnp.concatenate([rim_x[:, cols], x_ref[rows, cols]], axis=0)
-        else:
-            window = x_ref[pl.ds(b * BLOCK - RIM, BLOCK + RIM), cols]
-        value = conv(window.astype(F32), cx_ref[:, cols], bx_ref[:, cols])
-        xc[rows, cols] = value
-        us[rows, cols] = (value.astype(F32) * en[rows, cols]).astype(BF16)
 
     def conv_bc(b):
         rows = pl.ds(b * BLOCK, BLOCK)
@@ -137,18 +138,8 @@
         bcc[rows, :] = value
         bt[:, b * BLOCK : (b + 1) * BLOCK] = value[:, :n_state].astype(F32).T.astype(BF16)
 
-    def later_blocks(j, _):
-        for b in range(1, blocks):
-            conv_x(j, b)
-        return 0
-
-    def first_block(j, _):
-        conv_x(j, 0)
-        return 0
-
     for b in range(1, blocks):
         conv_bc(b)
-    lax.fori_loop(0, width // BLOCK, later_blocks, 0)
 
     @pl.when(ctx == 0)
     def _():
@@ -161,11 +152,38 @@
             copy.wait_recv()
 
     conv_bc(0)
-    lax.fori_loop(0, width // BLOCK, first_block, 0)
-
-    x_copies = {}
-    for g in range(groups):
-        cols = slice(g * GROUP, (g + 1) * GROUP)
+
+    @pl.when(iz == 0)
+    def _():
+        pz[...] = jnp.zeros_like(pz)
+
+    def x_copy(r, g):
+        return remote(
+            states.at[n_x - 1, :, span_of(g)], states.at[r - 1, :, span_of(g)],
+            x_send.at[r - 1, g], x_recv.at[r - 1, g],
+            iz * n_x + (ix + r) % n_x, tp,
+        )
+
+    def z_copy(g):
+        return remote(pz_next.at[:, span_of(g)], pz.at[:, span_of(g)], z_send.at[g], z_recv.at[g], ctx + n_x, tp)
+
+    def n_copy(g):
+        return remote(own_n.at[:, span_of(g)], sib_n.at[:, span_of(g)], n_send.at[g], n_recv.at[g], ctx, sib)
+
+    def own_state(g):
+        load_x(g).wait()
+        for half in range(GROUP // BLOCK):
+            cols = pl.ds(pl.multiple_of(g * GROUP + half * BLOCK, BLOCK), BLOCK)
+            for b in range(blocks):
+                rows = pl.ds(b * BLOCK, BLOCK)
+                if b == 0:
+                    window = jnp.concatenate([rim_x[:, cols], x_ref[rows, cols]], axis=0)
+                else:
+                    window = x_ref[pl.ds(b * BLOCK - RIM, BLOCK + RIM), cols]
+                value = conv(window.astype(F32), cx_ref[:, cols], bx_ref[:, cols])
+                xc[rows, cols] = value
+                us[rows, cols] = (value.astype(F32) * en[rows, cols]).astype(BF16)
+        cols = span_of(g)
         total = ec[toks - 1 : toks, cols]
         state = jnp.dot(bt[...], us[:, cols], preferred_element_type=F32)
         states[n_x - 1, :n_state, cols] = (state * total).astype(BF16)
@@ -173,47 +191,36 @@
         pick = lax.broadcasted_iota(jnp.int32, (RIM, GROUP), 0) < 8
         states[n_x - 1, n_state:, cols] = jnp.where(pick, high, total - high).astype(BF16)
         for r in range(1, n_x):
-            x_copies[r, g] = remote(
-                states.at[n_x - 1, :, pl.ds(g * GROUP, GROUP)],
-                states.at[r - 1, :, pl.ds(g * GROUP, GROUP)],
-                x_send.at[r - 1, g], x_recv.at[r - 1, g],
-                iz * n_x + (ix + r) % n_x, tp,
+            x_copy(r, g).start()
+
+    def score():
+        load_z.wait()
+        for b in range(blocks):
+            rows = slice(b * BLOCK, (b + 1) * BLOCK)
+            upto = (b + 1) * BLOCK
+            scores = lax.dot_general(
+                bcc[rows, n_state:], bcc[:upto, :n_state], (((1,), (1,)), ((), ())), preferred_element_type=F32
             )
-            x_copies[r, g].start()
+            pm[rows, :upto] = (scores * tril[rows, :upto].astype(F32)).astype(BF16)
 
     scale = 1.0 / math.sqrt(n_state * seq)
-    for b in range(blocks):
-        rows = slice(b * BLOCK, (b + 1) * BLOCK)
-        upto = (b + 1) * BLOCK
-        scores = lax.dot_general(
-            bcc[rows, n_state:], bcc[:upto, :n_state], (((1,), (1,)), ((), ())), preferred_element_type=F32
-        )
-        scores = (scores * tril[rows, :upto].astype(F32)).astype(BF16)
-
-        def inside(j, _, rows=rows, upto=upto, scores=scores):
-            cols = pl.ds(pl.multiple_of(j * GROUP, GROUP), GROUP)
-            y = jnp.dot(scores, us[:upto, cols], preferred_element_type=F32)
+
+    def inside(g):
+        cols = span_of(g)
+        for b in range(blocks):
+            rows = slice(b * BLOCK, (b + 1) * BLOCK)
+            upto = (b + 1) * BLOCK
+            y = jnp.dot(pm[rows, :upto], us[:upto, cols], preferred_element_type=F32)
             gate = silu(z_ref[rows, cols].astype(F32))
             decay = ec[rows, cols] * (scale * gate)
             g_all[rows, cols] = y * decay + skips[0:1, cols] * xc[rows, cols].astype(F32) * gate
             h_all[rows, cols] = decay
-            return 0
-
-        lax.fori_loop(0, groups, inside, 0)
-
-    @pl.when(iz == 0)
-    def _():
-        pz[...] = jnp.zeros_like(pz)
-
-    z_copies = []
-    for g in range(groups):
-        cols = slice(g * GROUP, (g + 1) * GROUP)
-        span = pl.ds(g * GROUP, GROUP)
-        copy = remote(pz_next.at[:, span], pz.at[:, span], z_send.at[g], z_recv.at[g], ctx + n_x, tp)
-        z_copies.append(copy)
+
+    def prefix(g):
+        cols = span_of(g)
         for r in range(1, n_x):
-            x_copies[r, g].wait_recv()
-        pl.when(iz > 0)(copy.wait_recv)
+            x_copy(r, g).wait_recv()
+        pl.when(iz > 0)(lambda: z_copy(g).wait_recv())
         before = pz[:, cols].astype(F32)
         arrived = before
         for k in range(n_x):
@@ -223,31 +230,34 @@
             factor = factor + states[slot, n_state + 8 : n_state + 9, cols].astype(F32)
             before = before * factor + states[slot, :n_state, cols].astype(F32)
         pz_next[:, cols] = before.astype(BF16)
-        pl.when(iz < n_z - 1)(copy.start)
+        pl.when(iz < n_z - 1)(lambda: z_copy(g).start())
         pin[:, cols] = arrived.astype(BF16)
 
-    n_copies = []
-    for b in range(blocks):
-        span = pl.ds(b * BLOCK, BLOCK)
-        n_copies.append(remote(own_n.at[span], sib_n.at[span], n_send.at[b], n_recv.at[b], ctx, sib))
-
-    def norm(b):
-        rows = slice(b * BLOCK, (b + 1) * BLOCK)
-
-        def pair(j, _):
-            start = pl.multiple_of(j * GROUP, GROUP)
-            cols = pl.ds(start, GROUP)
+    def norm(g):
+        cols = span_of(g)
+        for b in range(blocks):
+            rows = slice(b * BLOCK, (b + 1) * BLOCK)
             carried = jnp.dot(bcc[rows, n_state:], pin[:, cols], preferred_element_type=F32)
             gated = g_all[rows, cols] + h_all[rows, cols] * carried
             for half in range(GROUP // BLOCK):
                 piece = gated[:, half * BLOCK : (half + 1) * BLOCK]
                 mean_square = jnp.mean(piece * piece, axis=-1, keepdims=True)
-                cut = pl.ds(pl.multiple_of(start + half * BLOCK, BLOCK), BLOCK)
+                cut = pl.ds(pl.multiple_of(g * GROUP + half * BLOCK, BLOCK), BLOCK)
                 own_n[rows, cut] = (piece * lax.rsqrt(mean_square + 1e-05) * gain_ref[:, cut]).astype(BF16)
-            return 0
-
-        lax.fori_loop(0, groups, pair, 0)
-        n_copies[b].start()
+        n_copy(g).start()
+
+    delay = jnp.where(iz == n_z - 1, 2 * groups - 1, iz + 1)
+    late = jnp.maximum(delay, groups)
+
+    def slot_step(s, _):
+        pl.when(s < groups)(lambda: own_state(s))
+        pl.when(s == groups)(score)
+        pl.when((s >= groups) & (s < 2 * groups))(lambda: inside(s - groups))
+        pl.when((s >= delay) & (s < delay + groups))(lambda: prefix(s - delay))
+        pl.when((s >= late) & (s < late + groups))(lambda: norm(s - late))
+        return 0
+
+    lax.fori_loop(0, groups + max(2 * groups - 1, n_z), slot_step, 0)
 
     def project(b, r, first, tiles, store):
         rows = slice(b * BLOCK, (b + 1) * BLOCK)
@@ -264,7 +274,6 @@
     y_copies = {}
 
     def send_block(b):
-        n_copies[b].wait_recv()
         for r in range(1, n_y):
             if b == 0:
                 w_loads[r].wait()
@@ -272,22 +281,21 @@
             for p in range(parts):
 
                 def store(rows, j, cols, value, r=r, p=p):
-                    y_send[r - 1, p, rows, pl.ds(pl.multiple_of(j * GROUP, GROUP), GROUP)] = value.astype(BF16)
+                    y_send[r - 1, p, rows, span_of(j)] = value.astype(BF16)
 
                 project(b, r, p * part, part // GROUP, store)
                 span = pl.ds(b * BLOCK, BLOCK)
-                at = (b * parts + p,)
+                at = b * parts + p
                 y_copies[b, r, p] = remote(
                     y_send.at[r - 1, p, span], y_recv.at[r - 1, p, span],
-                    ys_send.at[r - 1, at[0]], ys_recv.at[r - 1, at[0]],
+                    ys_send.at[r - 1, at], ys_recv.at[r - 1, at],
                     ctx, (iy + r) % n_y * 2 + core,
                 )
                 y_copies[b, r, p].start()
 
-    norm(0)
+    for g in range(groups):
+        n_copy(g).wait_recv()
     for b in range(blocks):
-        if b + 1 < blocks:
-            norm(b + 1)
         send_block(b)
 
     w_loads[0].wait()
@@ -316,10 +324,14 @@
 
     @pl.when(iz < n_z - 1)
     def _():
-        for copy in z_copies:
-            copy.wait_send()
-
-    for copies in (w_swaps.values(), x_copies.values(), n_copies, y_copies.values()):
+        for g in range(groups):
+            z_copy(g).wait_send()
+
+    for g in range(groups):
+        n_copy(g).wait_send()
+        for r in range(1, n_x):
+            x_copy(r, g).wait_send()
+    for copies in (w_swaps.values(), y_copies.values()):
         for copy in copies:
             copy.wait_send()
 
@@ -341,16 +353,19 @@
         groups = width // GROUP
         blocks = toks // BLOCK
         vmem = pl.BlockSpec(memory_space=pltpu.VMEM)
+        hbm = pl.BlockSpec(memory_space=pl.ANY)
         smem = pl.BlockSpec(memory_space=pltpu.SMEM)
         dma = pltpu.SemaphoreType.DMA
         pieces = blocks * (owned // part)
         return pl.pallas_call(
             functools.partial(layer, n_ctx, n_tp, n_x),
             out_shape=jax.ShapeDtypeStruct((toks, owned), BF16),
-            in_specs=[vmem, vmem, vmem, vmem, smem, vmem, vmem, vmem, vmem, smem, vmem,
-                      pl.BlockSpec(memory_space=pl.ANY)],
+            in_specs=[hbm, vmem, hbm, vmem, smem, vmem, vmem, vmem, vmem, smem, vmem, hbm],
             out_specs=vmem,
             scratch_shapes=[
+                pltpu.VMEM((toks, width), BF16),
+                pltpu.VMEM((toks, width), BF16),
+                pltpu.VMEM((toks, toks), BF16),
                 pltpu.VMEM((RIM, width), BF16),
                 pltpu.VMEM((RIM, maps), BF16),
                 pltpu.VMEM((toks, toks), BF16),
@@ -376,17 +391,17 @@
                 pltpu.VMEM((far, owned // part, toks, part), BF16),
                 pltpu.VMEM((far, owned // part, toks, part), BF16),
                 pltpu.VMEM((toks, owned), F32),
-                dma((2,)), dma((2,)),
+                dma((groups,)), dma((1,)), dma((2,)), dma((2,)),
                 dma((n_y,)), dma((n_y,)), dma((n_y,)),
                 dma((row, groups)), dma((row, groups)),
                 dma((groups,)), dma((groups,)),
-                dma((blocks,)), dma((blocks,)),
+                dma((groups,)), dma((groups,)),
                 dma((far, pieces)), dma((far, pieces)),
             ],
             compiler_params=pltpu.CompilerParams(
                 collective_id=0, has_side_effects=True, vmem_limit_bytes=60 * 1024 * 1024
             ),
-        )(x_in, bc_in, z_in, codes, head_rate, conv_x, conv_bc, bias_x[None], bias_bc[None], skip,
+        )(x_in, bc_in, z_in, codes.T, head_rate, conv_x, conv_bc, bias_x[None], bias_bc[None], skip,
           norm_gain[None], w_out)
 
     in_specs = (

time: 83 us -> 78.8 us (0.949)
  Pallas kernels: 77.9 us -> 75.5 us
  local copies, waits for them, and re-layouts: 4.71 us -> 3.16 us
    pallas_call x1, Pallas kernels: 77.9 us -> 75.5 us  [body(): pl.pallas_call(functools.partial(layer, n_ctx, n_tp, n_x), out_shape=jax....]
    unnamed x2 -> x1, local copies, waits for them, and re-layouts: 4.71 us -> 3.16 us
where the time goes in v2:
time: 78.8 us; the launch traced here: 78.6 us
  Pallas kernels  75.5 us (96%)
  local copies, waits for them, and re-layouts  3.16 us (4%)
    pallas_call x1, Pallas kernels, body(): pl.pallas_call(functools.partial(layer, n_ctx, n_tp, n_x), out_shape=jax....  75.5 us
    unnamed x1, local copies, waits for them, and re-layouts  3.16 us

profile of v2, /device:TPU:27, one launch (start us, length us, event | category | flops | bytes accessed | tf_op | source)
XLA Modules:
  0.0 78.6 jit_solution(17219351253964549286)
XLA Ops:
  0.0 75.5 %shard_map.118 = bf16[512,2048]{1,0:T(8,128)(2,1)} custom-call(bf16[512,1024]{1,0:T(8,128)(2,1)} %x_hbm.1, bf16[512,256]{1,0:T(8,128)(2,1)} %bc_ref.1, bf16[512,1024]{1,0:T(8,128)(2,1)} %z_hbm.1, s32[8,512]{1,0:T(8,128)} %bitcast.4, f32[8]{0:T(128)} %rate_ref.1, f32[4,1024]{1,0:T(4,128)} %cx_ref.1, f32[4,256]{1,0:T(4,128)} %cbc_ref.1, f32[1,1024]{1,0:T(1,128)} %bitcast.5, ...), custom_call_target="tpu_custom_call" | custom-call | tf_op jit(solution)/shard_map/pallas_call | solution.py:360
  75.5 3.2 %copy.14 = bf16[512,2048]{1,0:T(8,128)(2,1)} copy(bf16[512,2048]{1,0:T(8,128)(2,1)} %shard_map.118) | data formatting | bytes 4194304

commit v3 on v2

--- a/solution.py
+++ b/solution.py
@@ -17,7 +17,8 @@
 
 
 def silu(v):
-    return v / (1.0 + jnp.exp(-v))
+    half = 0.5 * v
+    return half + half * jnp.tanh(half)
 
 
 def conv(window, taps, bias):
@@ -157,18 +158,22 @@
     def _():
         pz[...] = jnp.zeros_like(pz)
 
-    def x_copy(r, g):
+    def strip_of(q):
+        return pl.ds(pl.multiple_of(q * BLOCK, BLOCK), BLOCK)
+
+    def x_copy(r, q):
         return remote(
-            states.at[n_x - 1, :, span_of(g)], states.at[r - 1, :, span_of(g)],
-            x_send.at[r - 1, g], x_recv.at[r - 1, g],
+            states.at[n_x - 1, :, strip_of(q)], states.at[r - 1, :, strip_of(q)],
+            x_send.at[r - 1, q], x_recv.at[r - 1, q],
             iz * n_x + (ix + r) % n_x, tp,
         )
 
-    def z_copy(g):
-        return remote(pz_next.at[:, span_of(g)], pz.at[:, span_of(g)], z_send.at[g], z_recv.at[g], ctx + n_x, tp)
-
-    def n_copy(g):
-        return remote(own_n.at[:, span_of(g)], sib_n.at[:, span_of(g)], n_send.at[g], n_recv.at[g], ctx, sib)
+    def z_copy(q):
+        return remote(pz_next.at[:, strip_of(q)], pz.at[:, strip_of(q)], z_send.at[q], z_recv.at[q], ctx + n_x, tp)
+
+    def n_copy(g, b):
+        rows = pl.ds(b * BLOCK, BLOCK)
+        return remote(own_n.at[rows, span_of(g)], sib_n.at[rows, span_of(g)], n_send.at[g, b], n_recv.at[g, b], ctx, sib)
 
     def own_state(g):
         load_x(g).wait()
@@ -190,8 +195,9 @@
         high = total.astype(BF16).astype(F32)
         pick = lax.broadcasted_iota(jnp.int32, (RIM, GROUP), 0) < 8
         states[n_x - 1, n_state:, cols] = jnp.where(pick, high, total - high).astype(BF16)
-        for r in range(1, n_x):
-            x_copy(r, g).start()
+        for half in range(GROUP // BLOCK):
+            for r in range(1, n_x):
+                x_copy(r, g * (GROUP // BLOCK) + half).start()
 
     def score():
         load_z.wait()
@@ -217,21 +223,23 @@
             h_all[rows, cols] = decay
 
     def prefix(g):
-        cols = span_of(g)
-        for r in range(1, n_x):
-            x_copy(r, g).wait_recv()
-        pl.when(iz > 0)(lambda: z_copy(g).wait_recv())
-        before = pz[:, cols].astype(F32)
-        arrived = before
-        for k in range(n_x):
-            slot = (ix - k - 1 + n_x) % n_x
-            arrived = jnp.where(ix == k, before, arrived)
-            factor = states[slot, n_state : n_state + 1, cols].astype(F32)
-            factor = factor + states[slot, n_state + 8 : n_state + 9, cols].astype(F32)
-            before = before * factor + states[slot, :n_state, cols].astype(F32)
-        pz_next[:, cols] = before.astype(BF16)
-        pl.when(iz < n_z - 1)(lambda: z_copy(g).start())
-        pin[:, cols] = arrived.astype(BF16)
+        for half in range(GROUP // BLOCK):
+            q = g * (GROUP // BLOCK) + half
+            cols = strip_of(q)
+            for r in range(1, n_x):
+                x_copy(r, q).wait_recv()
+            pl.when(iz > 0)(functools.partial(lambda q: z_copy(q).wait_recv(), q))
+            before = pz[:, cols].astype(F32)
+            arrived = before
+            for k in range(n_x):
+                slot = (ix - k - 1 + n_x) % n_x
+                arrived = jnp.where(ix == k, before, arrived)
+                factor = states[slot, n_state : n_state + 1, cols].astype(F32)
+                factor = factor + states[slot, n_state + 8 : n_state + 9, cols].astype(F32)
+                before = before * factor + states[slot, :n_state, cols].astype(F32)
+            pz_next[:, cols] = before.astype(BF16)
+            pl.when(iz < n_z - 1)(functools.partial(lambda q: z_copy(q).start(), q))
+            pin[:, cols] = arrived.astype(BF16)
 
     def norm(g):
         cols = span_of(g)
@@ -244,7 +252,7 @@
                 mean_square = jnp.mean(piece * piece, axis=-1, keepdims=True)
                 cut = pl.ds(pl.multiple_of(g * GROUP + half * BLOCK, BLOCK), BLOCK)
                 own_n[rows, cut] = (piece * lax.rsqrt(mean_square + 1e-05) * gain_ref[:, cut]).astype(BF16)
-        n_copy(g).start()
+            n_copy(g, b).start()
 
     delay = jnp.where(iz == n_z - 1, 2 * groups - 1, iz + 1)
     late = jnp.maximum(delay, groups)
@@ -293,9 +301,9 @@
                 )
                 y_copies[b, r, p].start()
 
-    for g in range(groups):
-        n_copy(g).wait_recv()
     for b in range(blocks):
+        for g in range(groups):
+            n_copy(g, b).wait_recv()
         send_block(b)
 
     w_loads[0].wait()
@@ -324,16 +332,31 @@
 
     @pl.when(iz < n_z - 1)
     def _():
-        for g in range(groups):
-            z_copy(g).wait_send()
+        for q in range(width // BLOCK):
+            z_copy(q).wait_send()
 
     for g in range(groups):
-        n_copy(g).wait_send()
+        for b in range(blocks):
+            n_copy(g, b).wait_send()
+    for q in range(width // BLOCK):
         for r in range(1, n_x):
-            x_copy(r, g).wait_send()
+            x_copy(r, q).wait_send()
     for copies in (w_swaps.values(), y_copies.values()):
         for copy in copies:
             copy.wait_send()
+
+
+def hand_on(from_ref, to_ref, sem):
+    count = sem.shape[0]
+    rows = from_ref.shape[0] // count
+    copies = []
+    for k in range(count):
+        span = pl.ds(k * rows, rows)
+        copies.append(pltpu.make_async_copy(from_ref.at[span], to_ref.at[span], sem.at[k]))
+    for copy in copies:
+        copy.start()
+    for copy in copies:
+        copy.wait()
 
 
 def solution(mesh):
@@ -346,20 +369,21 @@
         n_state = maps // 2
         depth, model = w_out.shape
         owned = model // n_tp
-        part = min(owned, 1024)
+        part = min(owned, 512)
         n_y = n_tp // 2
         far = max(1, n_y - 1)
         row = max(1, n_x - 1)
         groups = width // GROUP
+        strips = width // BLOCK
         blocks = toks // BLOCK
         vmem = pl.BlockSpec(memory_space=pltpu.VMEM)
         hbm = pl.BlockSpec(memory_space=pl.ANY)
         smem = pl.BlockSpec(memory_space=pltpu.SMEM)
         dma = pltpu.SemaphoreType.DMA
         pieces = blocks * (owned // part)
-        return pl.pallas_call(
+        result = pl.pallas_call(
             functools.partial(layer, n_ctx, n_tp, n_x),
-            out_shape=jax.ShapeDtypeStruct((toks, owned), BF16),
+            out_shape=pltpu.VMEM((toks, owned), BF16),
             in_specs=[hbm, vmem, hbm, vmem, smem, vmem, vmem, vmem, vmem, smem, vmem, hbm],
             out_specs=vmem,
             scratch_shapes=[
@@ -393,16 +417,23 @@
                 pltpu.VMEM((toks, owned), F32),
                 dma((groups,)), dma((1,)), dma((2,)), dma((2,)),
                 dma((n_y,)), dma((n_y,)), dma((n_y,)),
-                dma((row, groups)), dma((row, groups)),
-                dma((groups,)), dma((groups,)),
-                dma((groups,)), dma((groups,)),
+                dma((row, strips)), dma((row, strips)),
+                dma((strips,)), dma((strips,)),
+                dma((groups, blocks)), dma((groups, blocks)),
                 dma((far, pieces)), dma((far, pieces)),
             ],
             compiler_params=pltpu.CompilerParams(
-                collective_id=0, has_side_effects=True, vmem_limit_bytes=60 * 1024 * 1024
+                collective_id=0, has_side_effects=True, vmem_limit_bytes=58 * 1024 * 1024
             ),
         )(x_in, bc_in, z_in, codes.T, head_rate, conv_x, conv_bc, bias_x[None], bias_bc[None], skip,
           norm_gain[None], w_out)
+        return pl.pallas_call(
+            hand_on,
+            out_shape=jax.ShapeDtypeStruct((toks, owned), BF16),
+            in_specs=[pl.BlockSpec(memory_space=pltpu.VMEM)],
+            out_specs=hbm,
+            scratch_shapes=[dma((8,))],
+        )(result)
 
     in_specs = (
         P("ctx", "tp"), P("ctx", None), P("ctx", "tp"), P("ctx", "tp"), P("tp"), P(None, "tp"),

time: 78.8 us -> 78.1 us (level)
  local copies, waits for them, and re-layouts: 3.16 us -> 1.34 us
  Pallas kernels: 75.5 us -> 76.6 us
    unnamed x1 -> x2, local copies, waits for them, and re-layouts: 3.16 us -> 1.34 us
    pallas_call x1 -> x2, Pallas kernels: 75.5 us -> 76.6 us  [the longest x1 73.6 us: body(): pl.pallas_call(functools.partial(layer, n_ctx, n_tp, n_x), out_shape=pltp...]
where the time goes in v3:
time: 78.1 us; the launch traced here: 77.9 us
  Pallas kernels  76.6 us (98%)
  local copies, waits for them, and re-layouts  1.34 us (2%)
    pallas_call x1, Pallas kernels, body(): pl.pallas_call(functools.partial(layer, n_ctx, n_tp, n_x), out_shape=pltp...  73.6 us
    pallas_call x1, Pallas kernels, body(): pl.pallas_call(hand_on, out_shape=jax.ShapeDtypeStruct((toks, owned), BF1...  2.96 us

profile of v3, /device:TPU:27, one launch (start us, length us, event | category | flops | bytes accessed | tf_op | source)
XLA Modules:
  0.0 77.9 jit_solution(4489984922309741834)
XLA Ops:
  0.0 73.6 %shard_map.118.from_ref = bf16[512,2048]{1,0:T(8,128)(2,1)S(1)} custom-call(bf16[512,1024]{1,0:T(8,128)(2,1)} %x_hbm.1, bf16[512,256]{1,0:T(8,128)(2,1)} %bc_ref.1, bf16[512,1024]{1,0:T(8,128)(2,1)} %z_hbm.1, s32[8,512]{1,0:T(8,128)} %bitcast.4, f32[8]{0:T(128)} %rate_ref.1, f32[4,1024]{1,0:T(4,128)} %cx_ref.1, f32[4,256]{1,0:T(4,128)} %cbc_ref.1, ...), custom_call_target="tpu_custom_call" | custom-call | tf_op jit(solution)/shard_map/pallas_call | solution.py:384
  73.6 0.0 copy-start
  73.6 1.3 %copy-done = bf16[512,2048]{1,0:T(8,128)(2,1)} copy-done((bf16[512,2048]{1,0:T(8,128)(2,1)}, bf16[512,2048]{1,0:T(8,128)(2,1)S(1)}, u32[]{:S(2)}) %copy-start) | copy-done | bytes 2097176
  75.0 3.0 %shard_map.119 = bf16[512,2048]{1,0:T(8,128)(2,1)} custom-call(bf16[512,2048]{1,0:T(8,128)(2,1)} %copy-done), custom_call_target="tpu_custom_call" | custom-call | tf_op jit(solution)/shard_map/pallas_call | solution.py:430
Async XLA Ops:
  73.6 1.3 %copy-start = (bf16[512,2048]{1,0:T(8,128)(2,1)}, bf16[512,2048]{1,0:T(8,128)(2,1)S(1)}, u32[]{:S(2)}) copy-start(bf16[512,2048]{1,0:T(8,128)(2,1)S(1)} %shard_map.118.from_ref) | copy-start | bytes 6291460

commit v4 on v3

--- a/solution.py
+++ b/solution.py
@@ -109,16 +109,17 @@
         for copy in rims:
             copy.start()
 
-    order = list(range(1, n_y)) + [0]
-    w_loads, w_swaps = {}, {}
-    for r in order:
-        chip = (iy + r) % n_y
-        mine = pl.ds(pl.multiple_of((chip * 2 + core) * owned, GROUP), owned)
-        theirs = pl.ds(pl.multiple_of((chip * 2 + 1 - core) * owned, GROUP), owned)
-        w_loads[r] = pltpu.make_async_copy(w_ref.at[:, mine], w_own.at[r], wl_sem.at[r])
-        w_swaps[r] = remote(w_ref.at[:, theirs], w_sib.at[r], ws_send.at[r], ws_recv.at[r], ctx, sib)
-        w_loads[r].start()
-        w_swaps[r].start()
+    chunks = owned // GROUP
+
+    def w_load(r):
+        first = pl.multiple_of(((iy + r) % n_y * 2 + core) * owned, GROUP)
+        return pltpu.make_async_copy(w_ref.at[:, pl.ds(first, owned)], w_own.at[r], wl_sem.at[r])
+
+    def w_swap(r, c):
+        first = pl.multiple_of(((iy + r) % n_y * 2 + 1 - core) * owned + c * GROUP, GROUP)
+        return remote(
+            w_ref.at[:, pl.ds(first, GROUP)], w_sib.at[r, :, span_of(c)], ws_send.at[r, c], ws_recv.at[r, c], ctx, sib
+        )
 
     def decays(j, _):
         cols = span_of(j)
@@ -254,18 +255,30 @@
                 own_n[rows, cut] = (piece * lax.rsqrt(mean_square + 1e-05) * gain_ref[:, cut]).astype(BF16)
             n_copy(g, b).start()
 
-    delay = jnp.where(iz == n_z - 1, 2 * groups - 1, iz + 1)
+    delay = jnp.where(iz == n_z - 1, 2 * groups, iz + 1)
     late = jnp.maximum(delay, groups)
+
+    slots = groups + max(2 * groups, n_z)
+    ahead = min(slots, (n_y - 1) * chunks)
+
+    def first_loads():
+        for r in range(1, n_y):
+            w_load(r).start()
 
     def slot_step(s, _):
         pl.when(s < groups)(lambda: own_state(s))
+        pl.when((s >= delay) & (s < delay + groups))(lambda: prefix(s - delay))
+        pl.when(s < ahead)(lambda: w_swap(1 + s // chunks, s % chunks).start())
+        pl.when(s == 1)(first_loads)
+        pl.when(s == groups)(lambda: w_load(0).start())
         pl.when(s == groups)(score)
         pl.when((s >= groups) & (s < 2 * groups))(lambda: inside(s - groups))
-        pl.when((s >= delay) & (s < delay + groups))(lambda: prefix(s - delay))
         pl.when((s >= late) & (s < late + groups))(lambda: norm(s - late))
         return 0
 
-    lax.fori_loop(0, groups + max(2 * groups - 1, n_z), slot_step, 0)
+    lax.fori_loop(0, slots, slot_step, 0)
+    for k in range(ahead, (n_y - 1) * chunks):
+        w_swap(1 + k // chunks, k % chunks).start()
 
     def project(b, r, first, tiles, store):
         rows = slice(b * BLOCK, (b + 1) * BLOCK)
@@ -281,12 +294,16 @@
 
     y_copies = {}
 
+    near = list(range(chunks))
+
     def send_block(b):
         for r in range(1, n_y):
             if b == 0:
-                w_loads[r].wait()
-                w_swaps[r].wait_recv()
+                w_load(r).wait()
             for p in range(parts):
+                if b == 0:
+                    for c in range(p * part // GROUP, (p + 1) * part // GROUP):
+                        w_swap(r, c).wait_recv()
 
                 def store(rows, j, cols, value, r=r, p=p):
                     y_send[r - 1, p, rows, span_of(j)] = value.astype(BF16)
@@ -300,14 +317,19 @@
                     ctx, (iy + r) % n_y * 2 + core,
                 )
                 y_copies[b, r, p].start()
+                if near:
+                    w_swap(0, near.pop(0)).start()
 
     for b in range(blocks):
         for g in range(groups):
             n_copy(g, b).wait_recv()
         send_block(b)
 
-    w_loads[0].wait()
-    w_swaps[0].wait_recv()
+    for c in near:
+        w_swap(0, c).start()
+    w_load(0).wait()
+    for c in range(chunks):
+        w_swap(0, c).wait_recv()
 
     def keep(rows, j, cols, value):
         local[rows, cols] = value
@@ -341,22 +363,11 @@
     for q in range(width // BLOCK):
         for r in range(1, n_x):
             x_copy(r, q).wait_send()
-    for copies in (w_swaps.values(), y_copies.values()):
-        for copy in copies:
-            copy.wait_send()
-
-
-def hand_on(from_ref, to_ref, sem):
-    count = sem.shape[0]
-    rows = from_ref.shape[0] // count
-    copies = []
-    for k in range(count):
-        span = pl.ds(k * rows, rows)
-        copies.append(pltpu.make_async_copy(from_ref.at[span], to_ref.at[span], sem.at[k]))
-    for copy in copies:
-        copy.start()
-    for copy in copies:
-        copy.wait()
+    for r in range(n_y):
+        for c in range(chunks):
+            w_swap(r, c).wait_send()
+    for copy in y_copies.values():
+        copy.wait_send()
 
 
 def solution(mesh):
@@ -381,7 +392,7 @@
         smem = pl.BlockSpec(memory_space=pltpu.SMEM)
         dma = pltpu.SemaphoreType.DMA
         pieces = blocks * (owned // part)
-        result = pl.pallas_call(
+        return pl.pallas_call(
             functools.partial(layer, n_ctx, n_tp, n_x),
             out_shape=pltpu.VMEM((toks, owned), BF16),
             in_specs=[hbm, vmem, hbm, vmem, smem, vmem, vmem, vmem, vmem, smem, vmem, hbm],
@@ -416,7 +427,7 @@
                 pltpu.VMEM((far, owned // part, toks, part), BF16),
                 pltpu.VMEM((toks, owned), F32),
                 dma((groups,)), dma((1,)), dma((2,)), dma((2,)),
-                dma((n_y,)), dma((n_y,)), dma((n_y,)),
+                dma((n_y,)), dma((n_y, owned // GROUP)), dma((n_y, owned // GROUP)),
                 dma((row, strips)), dma((row, strips)),
                 dma((strips,)), dma((strips,)),
                 dma((groups, blocks)), dma((groups, blocks)),
@@ -427,13 +438,6 @@
             ),
         )(x_in, bc_in, z_in, codes.T, head_rate, conv_x, conv_bc, bias_x[None], bias_bc[None], skip,
           norm_gain[None], w_out)
-        return pl.pallas_call(
-            hand_on,
-            out_shape=jax.ShapeDtypeStruct((toks, owned), BF16),
-            in_specs=[pl.BlockSpec(memory_space=pltpu.VMEM)],
-            out_specs=hbm,
-            scratch_shapes=[dma((8,))],
-        )(result)
 
     in_specs = (
         P("ctx", "tp"), P("ctx", None), P("ctx", "tp"), P("ctx", "tp"), P("tp"), P(None, "tp"),

time: 78.1 us -> 75.7 us (0.969)
  Pallas kernels: 76.6 us -> 74.2 us
    pallas_call x1 -> x0, Pallas kernels: 2.96 us -> none  [body(): pl.pallas_call(hand_on, out_shape=jax.ShapeDtypeStruct((toks, owned), BF1...]
where the time goes in v4:
time: 75.7 us; the launch traced here: 75.6 us
  Pallas kernels  74.2 us (98%)
  local copies, waits for them, and re-layouts  1.32 us (2%)
    pallas_call x1, Pallas kernels, body(): pl.pallas_call(functools.partial(layer, n_ctx, n_tp, n_x), out_shape=pltp...  74.2 us

profile of v4, /device:TPU:27, one launch (start us, length us, event | category | flops | bytes accessed | tf_op | source)
XLA Modules:
  0.0 75.6 jit_solution(4761026722757600834)
XLA Ops:
  0.0 74.2 %shard_map.118 = bf16[512,2048]{1,0:T(8,128)(2,1)S(1)} custom-call(bf16[512,1024]{1,0:T(8,128)(2,1)} %x_hbm.1, bf16[512,256]{1,0:T(8,128)(2,1)} %bc_ref.1, bf16[512,1024]{1,0:T(8,128)(2,1)} %z_hbm.1, s32[8,512]{1,0:T(8,128)} %bitcast.4, f32[8]{0:T(128)} %rate_ref.1, f32[4,1024]{1,0:T(4,128)} %cx_ref.1, f32[4,256]{1,0:T(4,128)} %cbc_ref.1, ...), custom_call_target="tpu_custom_call" | custom-call | tf_op jit(solution)/shard_map/pallas_call | solution.py:395
  74.2 1.3 %copy.14 = bf16[512,2048]{1,0:T(8,128)(2,1)} copy(bf16[512,2048]{1,0:T(8,128)(2,1)S(1)} %shard_map.118) | data formatting | bytes 4194304

commit v5 on v4

--- a/solution.py
+++ b/solution.py
@@ -34,7 +34,7 @@
     n_x,
     x_hbm, bc_ref, z_hbm, codes_ref, rate_ref, cx_ref, cbc_ref, bx_ref, bbc_ref, skip_ref, gain_ref, w_ref,
     out_ref,
-    x_ref, z_ref, pm, rim_x, rim_bc, tril, coded, coef, skips, ec, en, bcc, bt, xc, us, states, pz, pz_next, pin,
+    x_ref, z_ref, pm, rim_x, rim_bc, tril, coded, coef, skips, cum, bcc, bt, xc, us, states, pz, pz_next, pin,
     g_all, h_all, own_n, sib_n, w_own, w_sib, y_send, y_recv, local,
     xl_sem, zl_sem, rim_send, rim_recv, wl_sem, ws_send, ws_recv, x_send, x_recv, z_send, z_recv, n_send, n_recv, ys_send, ys_recv,
 ):
@@ -123,9 +123,7 @@
 
     def decays(j, _):
         cols = span_of(j)
-        cum = jnp.dot(tril[...], coded[:, cols], preferred_element_type=F32) * coef[0:1, cols]
-        ec[:, cols] = jnp.exp(cum)
-        en[:, cols] = jnp.exp(-cum)
+        cum[:, cols] = jnp.dot(tril[...], coded[:, cols], preferred_element_type=F32) * coef[0:1, cols]
         return 0
 
     lax.fori_loop(0, groups, decays, 0)
@@ -188,9 +186,9 @@
                     window = x_ref[pl.ds(b * BLOCK - RIM, BLOCK + RIM), cols]
                 value = conv(window.astype(F32), cx_ref[:, cols], bx_ref[:, cols])
                 xc[rows, cols] = value
-                us[rows, cols] = (value.astype(F32) * en[rows, cols]).astype(BF16)
+                us[rows, cols] = (value.astype(F32) * jnp.exp(-cum[rows, cols])).astype(BF16)
         cols = span_of(g)
-        total = ec[toks - 1 : toks, cols]
+        total = jnp.exp(cum[toks - 1 : toks, cols])
         state = jnp.dot(bt[...], us[:, cols], preferred_element_type=F32)
         states[n_x - 1, :n_state, cols] = (state * total).astype(BF16)
         high = total.astype(BF16).astype(F32)
@@ -219,7 +217,7 @@
             upto = (b + 1) * BLOCK
             y = jnp.dot(pm[rows, :upto], us[:upto, cols], preferred_element_type=F32)
             gate = silu(z_ref[rows, cols].astype(F32))
-            decay = ec[rows, cols] * (scale * gate)
+            decay = jnp.exp(cum[rows, cols]) * (scale * gate)
             g_all[rows, cols] = y * decay + skips[0:1, cols] * xc[rows, cols].astype(F32) * gate
             h_all[rows, cols] = decay
 
@@ -280,8 +278,7 @@
     for k in range(ahead, (n_y - 1) * chunks):
         w_swap(1 + k // chunks, k % chunks).start()
 
-    def project(b, r, first, tiles, store):
-        rows = slice(b * BLOCK, (b + 1) * BLOCK)
+    def project(rows, r, first, tiles, store):
 
         def tile(j, _):
             cols = pl.ds(pl.multiple_of(first + j * GROUP, GROUP), GROUP)
@@ -296,34 +293,37 @@
 
     near = list(range(chunks))
 
-    def send_block(b):
+    def send_rows(k, low, high):
+        rows = slice(low, high)
         for r in range(1, n_y):
-            if b == 0:
+            if k == 0:
                 w_load(r).wait()
             for p in range(parts):
-                if b == 0:
+                if k == 0:
                     for c in range(p * part // GROUP, (p + 1) * part // GROUP):
                         w_swap(r, c).wait_recv()
 
                 def store(rows, j, cols, value, r=r, p=p):
                     y_send[r - 1, p, rows, span_of(j)] = value.astype(BF16)
 
-                project(b, r, p * part, part // GROUP, store)
-                span = pl.ds(b * BLOCK, BLOCK)
-                at = b * parts + p
-                y_copies[b, r, p] = remote(
+                project(rows, r, p * part, part // GROUP, store)
+                span = pl.ds(low, high - low)
+                at = k * parts + p
+                y_copies[k, r, p] = remote(
                     y_send.at[r - 1, p, span], y_recv.at[r - 1, p, span],
                     ys_send.at[r - 1, at], ys_recv.at[r - 1, at],
                     ctx, (iy + r) % n_y * 2 + core,
                 )
-                y_copies[b, r, p].start()
+                y_copies[k, r, p].start()
                 if near:
                     w_swap(0, near.pop(0)).start()
 
-    for b in range(blocks):
-        for g in range(groups):
-            n_copy(g, b).wait_recv()
-        send_block(b)
+    stretches = [(0, BLOCK), (BLOCK, toks)]
+    for k, (low, high) in enumerate(stretches):
+        for b in range(low // BLOCK, high // BLOCK):
+            for g in range(groups):
+                n_copy(g, b).wait_recv()
+        send_rows(k, low, high)
 
     for c in near:
         w_swap(0, c).start()
@@ -334,16 +334,15 @@
     def keep(rows, j, cols, value):
         local[rows, cols] = value
 
-    for b in range(blocks):
-        project(b, 0, 0, owned // GROUP, keep)
-
-    for b in range(blocks):
-        rows = slice(b * BLOCK, (b + 1) * BLOCK)
+    project(slice(0, toks), 0, 0, chunks, keep)
+
+    for k, (low, high) in enumerate(stretches):
+        rows = slice(low, high)
         for p in range(parts):
             cols = slice(p * part, (p + 1) * part)
             total = local[rows, cols]
             for r in range(1, n_y):
-                y_copies[b, r, p].wait_recv()
+                y_copies[k, r, p].wait_recv()
                 total = total + y_recv[r - 1, p, rows, :].astype(F32)
             out_ref[rows, cols] = total.astype(BF16)
 
@@ -391,7 +390,7 @@
         hbm = pl.BlockSpec(memory_space=pl.ANY)
         smem = pl.BlockSpec(memory_space=pltpu.SMEM)
         dma = pltpu.SemaphoreType.DMA
-        pieces = blocks * (owned // part)
+        pieces = 2 * (owned // part)
         return pl.pallas_call(
             functools.partial(layer, n_ctx, n_tp, n_x),
             out_shape=pltpu.VMEM((toks, owned), BF16),
@@ -407,7 +406,6 @@
                 pltpu.VMEM((toks, width), BF16),
                 pltpu.VMEM((8, width), F32),
                 pltpu.VMEM((8, width), F32),
-                pltpu.VMEM((toks, width), F32),
                 pltpu.VMEM((toks, width), F32),
                 pltpu.VMEM((toks, maps), BF16),
                 pltpu.VMEM((n_state, toks), BF16),

time: 75.7 us -> 75.7 us (level)
  no operation moved by 1% of the time
where the time goes in v5:
time: 75.7 us; the launch traced here: 75.5 us
  Pallas kernels  74.2 us (98%)
  local copies, waits for them, and re-layouts  1.32 us (2%)
    pallas_call x1, Pallas kernels, body(): pl.pallas_call(functools.partial(layer, n_ctx, n_tp, n_x), out_shape=pltp...  74.2 us

profile of v5, /device:TPU:27, one launch (start us, length us, event | category | flops | bytes accessed | tf_op | source)
XLA Modules:
  0.0 75.5 jit_solution(5137702923808826717)
XLA Ops:
  0.0 74.2 %shard_map.118 = bf16[512,2048]{1,0:T(8,128)(2,1)S(1)} custom-call(bf16[512,1024]{1,0:T(8,128)(2,1)} %x_hbm.1, bf16[512,256]{1,0:T(8,128)(2,1)} %bc_ref.1, bf16[512,1024]{1,0:T(8,128)(2,1)} %z_hbm.1, s32[8,512]{1,0:T(8,128)} %bitcast.4, f32[8]{0:T(128)} %rate_ref.1, f32[4,1024]{1,0:T(4,128)} %cx_ref.1, f32[4,256]{1,0:T(4,128)} %cbc_ref.1, ...), custom_call_target="tpu_custom_call" | custom-call | tf_op jit(solution)/shard_map/pallas_call | solution.py:394
  74.2 1.3 %copy.14 = bf16[512,2048]{1,0:T(8,128)(2,1)} copy(bf16[512,2048]{1,0:T(8,128)(2,1)S(1)} %shard_map.118) | data formatting | bytes 4194304

commit v6 on v5

--- a/solution.py
+++ b/solution.py
@@ -210,9 +210,9 @@
 
     scale = 1.0 / math.sqrt(n_state * seq)
 
-    def inside(g):
+    def inside(g, some):
         cols = span_of(g)
-        for b in range(blocks):
+        for b in some:
             rows = slice(b * BLOCK, (b + 1) * BLOCK)
             upto = (b + 1) * BLOCK
             y = jnp.dot(pm[rows, :upto], us[:upto, cols], preferred_element_type=F32)
@@ -240,9 +240,9 @@
             pl.when(iz < n_z - 1)(functools.partial(lambda q: z_copy(q).start(), q))
             pin[:, cols] = arrived.astype(BF16)
 
-    def norm(g):
+    def norm(g, some):
         cols = span_of(g)
-        for b in range(blocks):
+        for b in some:
             rows = slice(b * BLOCK, (b + 1) * BLOCK)
             carried = jnp.dot(bcc[rows, n_state:], pin[:, cols], preferred_element_type=F32)
             gated = g_all[rows, cols] + h_all[rows, cols] * carried
@@ -270,8 +270,10 @@
         pl.when(s == 1)(first_loads)
         pl.when(s == groups)(lambda: w_load(0).start())
         pl.when(s == groups)(score)
-        pl.when((s >= groups) & (s < 2 * groups))(lambda: inside(s - groups))
-        pl.when((s >= late) & (s < late + groups))(lambda: norm(s - late))
+        local_turn = (s >= groups) & (s < 2 * groups)
+        pl.when(local_turn)(lambda: inside(s - groups, range(1)))
+        pl.when(local_turn & (iz == n_z - 1))(lambda: inside(s - groups, range(1, blocks)))
+        pl.when((s >= late) & (s < late + groups))(lambda: norm(s - late, range(1)))
         return 0
 
     lax.fori_loop(0, slots, slot_step, 0)
@@ -319,7 +321,14 @@
                     w_swap(0, near.pop(0)).start()
 
     stretches = [(0, BLOCK), (BLOCK, toks)]
+    def later_rows(g, _):
+        pl.when(iz < n_z - 1)(lambda: inside(g, range(1, blocks)))
+        norm(g, range(1, blocks))
+        return 0
+
     for k, (low, high) in enumerate(stretches):
+        if k == 1:
+            lax.fori_loop(0, groups, later_rows, 0)
         for b in range(low // BLOCK, high // BLOCK):
             for g in range(groups):
                 n_copy(g, b).wait_recv()

time: 75.7 us -> 74.5 us (0.984)
  Pallas kernels: 74.2 us -> 73 us
    pallas_call x1, Pallas kernels: 74.2 us -> 73 us  [body(): pl.pallas_call(functools.partial(layer, n_ctx, n_tp, n_x), out_shape=pltp...]
where the time goes in v6:
time: 74.5 us; the launch traced here: 74.3 us
  Pallas kernels  73 us (98%)
  local copies, waits for them, and re-layouts  1.32 us (2%)
    pallas_call x1, Pallas kernels, body(): pl.pallas_call(functools.partial(layer, n_ctx, n_tp, n_x), out_shape=pltp...  73 us

profile of v6, /device:TPU:27, one launch (start us, length us, event | category | flops | bytes accessed | tf_op | source)
XLA Modules:
  0.0 74.3 jit_solution(970051830679784420)
XLA Ops:
  0.0 73.0 %shard_map.118 = bf16[512,2048]{1,0:T(8,128)(2,1)S(1)} custom-call(bf16[512,1024]{1,0:T(8,128)(2,1)} %x_hbm.1, bf16[512,256]{1,0:T(8,128)(2,1)} %bc_ref.1, bf16[512,1024]{1,0:T(8,128)(2,1)} %z_hbm.1, s32[8,512]{1,0:T(8,128)} %bitcast.4, f32[8]{0:T(128)} %rate_ref.1, f32[4,1024]{1,0:T(4,128)} %cx_ref.1, f32[4,256]{1,0:T(4,128)} %cbc_ref.1, ...), custom_call_target="tpu_custom_call" | custom-call | tf_op jit(solution)/shard_map/pallas_call | solution.py:403
  73.0 1.3 %copy.14 = bf16[512,2048]{1,0:T(8,128)(2,1)} copy(bf16[512,2048]{1,0:T(8,128)(2,1)S(1)} %shard_map.118) | data formatting | bytes 4194304
